TPU v7x, 256 devices: a whole 4x4x8 slice. The times are simulated.
256 devices in a mesh: hist: 16 (over y, z_hi, core), mp: 16 (over x, z_lo).
Axes of the slice: x: 4, y: 4, z: 8 (z_hi: 2, z_lo: 4; z = z_hi * 4 + z_lo), core: 2. Of those that a mesh axis runs over, the one named last changes fastest.
Arguments:
- history_ids: int32 [8192], P('hist'), may hold values from 0 to 255
- latent_offsets: int32 [1024], P('hist'), may hold values from 0 to 8191, as said below
- byte_table: bfloat16 [256, 4096], replicated, may hold values from -6 to 6
- w_query: bfloat16 [4096, 4096], P(None, 'mp')
- w_key: bfloat16 [4096, 4096], P(None, 'mp')
- w_value: bfloat16 [4096, 4096], P(None, 'mp'), may hold values from -0.09375 to 0.09375
- w_out: bfloat16 [4096, 4096], P('mp'), may hold values from -0.125 to 0.125
- norm_gain: bfloat16 [4096], replicated, may hold values from 0.099609375 to 1.8984375
- w_self_query: bfloat16 [4096, 4096], P('hist', 'mp')
- w_self_key: bfloat16 [4096, 4096], P('hist', 'mp')
- w_self_value: bfloat16 [4096, 4096], P('hist', 'mp'), may hold values from -0.09375 to 0.09375
- w_self_out: bfloat16 [4096, 4096], P('mp', 'hist'), may hold values from -0.125 to 0.125
Outputs:
- latent_out: bfloat16 [1024, 4096], P('hist', 'mp')
Inputs may be any that keep to these rules, and one draw needn't show every extreme that they name: `latent_offsets`: strictly rising; latent i lies at or after position i * 8 and before (i + 1) * 8; the first is 0 and the last 8191.
All inputs are finite; a program needn't handle non-finite values.
Results may differ from a plain program's by a relative error of at most 0.035.
Values may be sent and summed in bfloat16 or wider, within the bound.
A program may use at most 64 MiB of HBM per device.

v0:
```python
import math

import jax
import jax.numpy as jnp
from jax import lax
from jax.sharding import PartitionSpec as P

HEAD_DIM = 128


def empty_state(row_count, head_count):
    return (
        jnp.full((head_count, row_count), -1e30, jnp.float32),
        jnp.zeros((head_count, row_count), jnp.float32),
        jnp.zeros((head_count, row_count, HEAD_DIM), jnp.float32),
    )


def attend_block(running, queries, limits, key_block, value_block, head_count):
    row_maxes, totals, weighted = running
    row_count = queries.shape[0]
    key_count = key_block.shape[0]
    query_heads = queries.reshape(row_count, head_count, HEAD_DIM)
    key_heads = key_block.reshape(key_count, head_count, HEAD_DIM)
    value_heads = value_block.reshape(key_count, head_count, HEAD_DIM)
    scores = jnp.einsum(
        "qhd,khd->hqk", query_heads, key_heads, preferred_element_type=jnp.float32
    ) * (1.0 / math.sqrt(HEAD_DIM))
    key_positions = jnp.arange(key_count, dtype=jnp.int32)
    allowed = key_positions[None, None, :] <= limits[None, :, None]
    scores = jnp.where(allowed, scores, -1e30)
    new_max = jnp.maximum(row_maxes, jnp.max(scores, axis=2))
    weights = jnp.where(allowed, jnp.exp(scores - new_max[:, :, None]), 0.0)
    totals = jnp.sum(weights, axis=2)
    weighted = jnp.einsum(
        "hqk,khd->hqd",
        weights.astype(jnp.bfloat16),
        value_heads,
        preferred_element_type=jnp.float32,
    )
    return (new_max, totals, weighted)


def finish(running):
    row_maxes, totals, weighted = running
    head_count, row_count = totals.shape
    context = weighted / totals[:, :, None]
    return context.transpose(1, 0, 2).reshape(row_count, head_count * HEAD_DIM).astype(jnp.bfloat16)


def per_device(
    history_ids,
    latent_offsets,
    byte_table,
    w_query,
    w_key,
    w_value,
    w_out,
    norm_gain,
    w_self_query,
    w_self_key,
    w_self_value,
    w_self_out,
):
    hist_index = lax.axis_index("hist")
    mp_index = lax.axis_index("mp")
    local_tokens = history_ids.shape[0]
    latent_count = latent_offsets.shape[0]
    share_width = w_key.shape[1]
    head_count = share_width // HEAD_DIM
    embedded = jnp.take(byte_table, history_ids, axis=0)
    hist_keys = jnp.dot(embedded, w_key, preferred_element_type=jnp.float32).astype(jnp.bfloat16)
    hist_values = jnp.dot(embedded, w_value, preferred_element_type=jnp.float32).astype(
        jnp.bfloat16
    )
    latent_embed = jnp.take(embedded, latent_offsets - hist_index * local_tokens, axis=0)
    latent_queries = jnp.dot(latent_embed, w_query, preferred_element_type=jnp.float32).astype(
        jnp.bfloat16
    )
    pieces = (
        lax.all_gather(hist_keys, "hist", axis=0, tiled=True),
        lax.all_gather(hist_values, "hist", axis=0, tiled=True),
    )
    running = attend_block(
        empty_state(latent_count, head_count),
        latent_queries,
        latent_offsets,
        pieces[0],
        pieces[1],
        head_count,
    )
    cross_ctx = finish(running)
    partial_value = jnp.dot(cross_ctx, w_out, preferred_element_type=jnp.float32)
    shared_part = lax.psum_scatter(
        partial_value.astype(jnp.bfloat16), "mp", scatter_dimension=1, tiled=True
    ).astype(jnp.float32)
    embed_slice = lax.dynamic_slice_in_dim(latent_embed, mp_index * share_width, share_width, 1)
    latent_part = (embed_slice.astype(jnp.float32) + shared_part).astype(jnp.bfloat16)
    latent_full = lax.all_gather(latent_part, "mp", axis=1, tiled=True)
    widened = latent_full.astype(jnp.float32)
    mean_square = jnp.mean(widened * widened, axis=1, keepdims=True)
    normed = (widened * lax.rsqrt(mean_square + 1e-05) * norm_gain.astype(jnp.float32)).astype(
        jnp.bfloat16
    )
    pieces = (
        lax.all_gather(w_self_query, "hist", axis=0, tiled=True),
        lax.all_gather(w_self_key, "hist", axis=0, tiled=True),
        lax.all_gather(w_self_value, "hist", axis=0, tiled=True),
    )
    self_q32, self_k32, self_v32 = tuple(
        (jnp.dot(normed, piece, preferred_element_type=jnp.float32) for piece in pieces)
    )
    self_queries = self_q32.astype(jnp.bfloat16)
    self_keys = self_k32.astype(jnp.bfloat16)
    self_values = self_v32.astype(jnp.bfloat16)
    latent_limits = hist_index * latent_count + jnp.arange(latent_count, dtype=jnp.int32)
    pieces = (
        lax.all_gather(self_keys, "hist", axis=0, tiled=True),
        lax.all_gather(self_values, "hist", axis=0, tiled=True),
    )
    self_state = attend_block(
        empty_state(latent_count, head_count),
        self_queries,
        latent_limits,
        pieces[0],
        pieces[1],
        head_count,
    )
    self_ctx = finish(self_state)
    out_terms = jnp.dot(
        self_ctx,
        lax.all_gather(w_self_out, "hist", axis=1, tiled=True),
        preferred_element_type=jnp.float32,
    )
    self_part = lax.psum_scatter(
        out_terms.astype(jnp.bfloat16), "mp", scatter_dimension=1, tiled=True
    ).astype(jnp.float32)
    return (latent_part.astype(jnp.float32) + self_part).astype(jnp.bfloat16)


def solution(mesh):
    return jax.shard_map(
        per_device,
        mesh=mesh,
        in_specs=(
            P("hist"),
            P("hist"),
            P(),
            P(None, "mp"),
            P(None, "mp"),
            P(None, "mp"),
            P("mp", None),
            P(),
            P("hist", "mp"),
            P("hist", "mp"),
            P("hist", "mp"),
            P("mp", "hist"),
        ),
        out_specs=P("hist", "mp"),
        check_vma=False,
    )
```

profile of v0, /device:TPU:1, one launch (start us, length us, event | category | flops | bytes accessed | tf_op | source)
XLA Modules:
  0.0 592.4 jit_solution(12586081295670752127)
XLA Ops:
  8.1 4.4 gather_fusion
  12.5 2.8 broadcast_select_fusion
  17.3 2.0 convolution_convert_fusion.3
  19.3 4.8 convolution_convert_fusion.2
  24.2 4.1 gather_fusion.1
  28.5 2.1 fusion.21
  30.9 70.0 %all-gather.7.cloned.1.call-done = bf16[8192,256]{1,0:T(8,128)(2,1)} async-done(((bf16[512,256]{1,0:T(8,128)(2,1)}), bf16[8192,256]{1,0:T(8,128)(2,1)}) %all-gather.7.cloned.1.call-update) | async-done | bytes 4194320 | tf_op jit(solution)/shard_map/all_gather | solution.py:81
  100.9 3.9 fusion.64
  104.9 2.0 copy-done.2
  108.0 68.4 %all-gather.9.cloned.1.call-done = bf16[8192,256]{1,0:T(8,128)(2,1)} async-done(((bf16[512,256]{1,0:T(8,128)(2,1)}), bf16[8192,256]{1,0:T(8,128)(2,1)}) %all-gather.9.cloned.1.call-update) | async-done | bytes 4194320 | tf_op jit(solution)/shard_map/all_gather | solution.py:82
  176.5 4.7 fusion.33
  185.2 65.3 %reduce-scatter.3.cloned.1.call-done = bf16[64,256]{1,0:T(8,128)(2,1)} async-done(((bf16[64,4096]{1,0:T(8,128)(2,1)}), bf16[64,256]{1,0:T(8,128)(2,1)}) %reduce-scatter.3.cloned.1.call-update) | async-done | bytes 32784 | tf_op jit(solution)/shard_map/reduce_scatter | solution.py:94
  251.3 36.8 %all_gather.29 = bf16[64,4096]{1,0:T(8,128)(2,1)S(1)} all-gather(bf16[64,256]{1,0:T(8,128)(2,1)S(1)} %add_convert_fusion.1), channel_id=1, replica_groups=mesh['hist'=16,'mp'=16] {'mp'}, dimensions={1}, use_global_device_ids=true | all-gather | bytes 557056 | tf_op jit(solution)/shard_map/all_gather | solution.py:99
  288.3 37.9 %all-gather.11.cloned.1.call-done = bf16[4096,256]{1,0:T(8,128)(2,1)} async-done(((bf16[256,256]{1,0:T(8,128)(2,1)}), bf16[4096,256]{1,0:T(8,128)(2,1)}) %all-gather.11.cloned.1.call-update) | async-done | bytes 2097168 | tf_op jit(solution)/shard_map/all_gather | solution.py:106
  326.2 2.1 fusion.22
  328.3 59.3 %all-gather.13.cloned.1.call-done = bf16[4096,256]{1,0:T(8,128)(2,1)} async-done(((bf16[256,256]{1,0:T(8,128)(2,1)}), bf16[4096,256]{1,0:T(8,128)(2,1)}) %all-gather.13.cloned.1.call-update) | async-done | bytes 2097168 | tf_op jit(solution)/shard_map/all_gather | solution.py:107
  387.6 2.1 convolution_convert_fusion.5
  389.7 28.6 %all_gather.32 = bf16[1024,256]{1,0:T(8,128)(2,1)S(1)} all-gather(bf16[64,256]{1,0:T(8,128)(2,1)S(1)} %convolution_convert_fusion.5), channel_id=1, replica_groups=mesh['hist'=16,'mp'=16] {'hist'}, dimensions={0}, use_global_device_ids=true | all-gather | bytes 557056 | tf_op jit(solution)/shard_map/all_gather | solution.py:118
  419.0 31.7 %all-gather.15.cloned.1.call-done = bf16[4096,256]{1,0:T(8,128)(2,1)} async-done(((bf16[256,256]{1,0:T(8,128)(2,1)}), bf16[4096,256]{1,0:T(8,128)(2,1)}) %all-gather.15.cloned.1.call-update) | async-done | bytes 2097168 | tf_op jit(solution)/shard_map/all_gather | solution.py:108
  450.7 2.1 convolution_convert_fusion.4
  452.8 28.6 %all_gather.34 = bf16[1024,256]{1,0:T(8,128)(2,1)S(1)} all-gather(bf16[64,256]{1,0:T(8,128)(2,1)S(1)} %convolution_convert_fusion.4), channel_id=1, replica_groups=mesh['hist'=16,'mp'=16] {'hist'}, dimensions={0}, use_global_device_ids=true | all-gather | bytes 557056 | tf_op jit(solution)/shard_map/all_gather | solution.py:119
  481.7 30.8 %all-gather.17.cloned.1.call-done = bf16[256,4096]{1,0:T(8,128)(2,1)} async-done(((bf16[256,256]{1,0:T(8,128)(2,1)}), bf16[256,4096]{1,0:T(8,128)(2,1)}) %all-gather.17.cloned.1.call-update) | async-done | bytes 2097168 | tf_op jit(solution)/shard_map/all_gather | solution.py:132
  512.5 2.9 convolution_convert_fusion
  515.4 68.8 %reduce-scatter.5.cloned.1.call-done = bf16[64,256]{1,0:T(8,128)(2,1)} async-done(((bf16[64,4096]{1,0:T(8,128)(2,1)}), bf16[64,256]{1,0:T(8,128)(2,1)}) %reduce-scatter.5.cloned.1.call-update) | async-done | bytes 32784 | tf_op jit(solution)/shard_map/reduce_scatter | solution.py:135
  (50 shorter events, 12.7 us)
Async XLA Ops:
  6.5 1.6 copy-start
  6.5 94.4 %all-gather.7.cloned.1.call-start = ((), (), s32[]{:S(2)}) async-start(), calls=%async_computation.2 | async-start | bytes 4456448 | tf_op jit(solution)/shard_map/all_gather | solution.py:81
  12.5 4.8 copy-start.6
  15.3 2.0 copy-start.1
  19.2 5.0 copy-start.5
  19.3 157.2 %all-gather.9.cloned.1.call-start = ((), (), s32[]{:S(2)}) async-start(), calls=%async_computation.3 | async-start | bytes 4456448 | tf_op jit(solution)/shard_map/all_gather | solution.py:82
  24.2 226.3 %reduce-scatter.3.cloned.1.call-start = ((), (), s32[]{:S(2)}) async-start(), calls=%async_computation.4 | async-start | bytes 557056 | tf_op jit(solution)/shard_map/reduce_scatter | solution.py:94
  104.8 2.0 copy-start.2
  176.5 4.7 copy-start.3
  176.5 8.6 %copy-start.4 = (bf16[4096]{0:T(1024)(128)(2,1)S(1)}, bf16[4096]{0:T(1024)(128)(2,1)}, u32[]{:S(2)}) copy-start(bf16[4096]{0:T(1024)(128)(2,1)} %param.19) | copy-start | bytes 24580
  182.6 143.6 %all-gather.11.cloned.1.call-start = ((), (), s32[]{:S(2)}) async-start(), calls=%async_computation.5 | async-start | bytes 2228224 | tf_op jit(solution)/shard_map/all_gather | solution.py:106
  183.1 204.5 %all-gather.13.cloned.1.call-start = ((), (), s32[]{:S(2)}) async-start(), calls=%async_computation.6 | async-start | bytes 2228224 | tf_op jit(solution)/shard_map/all_gather | solution.py:107
  183.7 266.9 %all-gather.15.cloned.1.call-start = ((), (), s32[]{:S(2)}) async-start(), calls=%async_computation.7 | async-start | bytes 2228224 | tf_op jit(solution)/shard_map/all_gather | solution.py:108
  184.3 328.2 %all-gather.17.cloned.1.call-start = ((), (), s32[]{:S(2)}) async-start(), calls=%async_computation.8 | async-start | bytes 2228224 | tf_op jit(solution)/shard_map/all_gather | solution.py:132
  185.0 399.1 %reduce-scatter.5.cloned.1.call-start = ((), (), s32[]{:S(2)}) async-start(), calls=%async_computation.9 | async-start | bytes 557056 | tf_op jit(solution)/shard_map/reduce_scatter | solution.py:135
Sparse Core Ops, SparseCore 0:
  19.4 81.5 all-gather.6
  103.6 72.8 all-gather.8
  182.7 67.7 reduce-scatter.2
  253.4 72.7 all-gather.10
  329.0 58.5 all-gather.12
  390.5 60.1 all-gather.14
  453.5 58.8 all-gather.16
  515.5 68.6 reduce-scatter.4
where the time goes:
time: 603 us; the launch traced here: 592 us
  waiting for transfers between devices  435 us (72%)
  blocking collectives  94 us (16%)
  matrix products  28.7 us (5%)
  between operations  13.7 us (2%)
  local copies, waits for them, and re-layouts  12.5 us (2%)
  other arithmetic  8.74 us (1%)
    all_gather x1, waiting for transfers between devices, per_device(): lax.all_gather(hist_keys, 'hist', axis=0, tiled=True)  70 us
    reduce_scatter x1, waiting for transfers between devices, per_device(): lax.psum_scatter(out_terms.astype(jnp.bfloat16), 'mp', scatter_dimension=...  68.8 us
    all_gather x1, waiting for transfers between devices, per_device(): lax.all_gather(hist_values, 'hist', axis=0, tiled=True)  68.4 us
    reduce_scatter x1, waiting for transfers between devices, per_device(): lax.psum_scatter(partial_value.astype(jnp.bfloat16), 'mp', scatter_dimens...  65.3 us
    all_gather x1, waiting for transfers between devices, per_device(): lax.all_gather(w_self_key, 'hist', axis=0, tiled=True)  59.3 us
    all_gather x1, waiting for transfers between devices, per_device(): lax.all_gather(w_self_query, 'hist', axis=0, tiled=True)  37.9 us
    all_gather x1, blocking collectives, per_device(): latent_full = lax.all_gather(latent_part, 'mp', axis=1, tiled=True)  36.8 us
    all_gather x1, waiting for transfers between devices, per_device(): lax.all_gather(w_self_value, 'hist', axis=0, tiled=True)  31.7 us
  transfers between devices with their start and end apart: 8, of which 8 were waited for; matrix products, arithmetic and copies ran while one was open for 4% of the time, Pallas kernels for 0%

commit v1 on v0

--- a/solution.py
+++ b/solution.py
@@ -68,28 +68,43 @@
     latent_count = latent_offsets.shape[0]
     share_width = w_key.shape[1]
     head_count = share_width // HEAD_DIM
-    embedded = jnp.take(byte_table, history_ids, axis=0)
-    hist_keys = jnp.dot(embedded, w_key, preferred_element_type=jnp.float32).astype(jnp.bfloat16)
-    hist_values = jnp.dot(embedded, w_value, preferred_element_type=jnp.float32).astype(
+    all_ids = lax.all_gather(history_ids, "hist", axis=0, tiled=True)
+    vocab = byte_table.shape[0]
+    vocab_ids = jnp.arange(vocab, dtype=jnp.int32)
+    token_hot = (all_ids[:, None] == vocab_ids[None, :]).astype(jnp.bfloat16)
+    places = jnp.arange(all_ids.shape[0], dtype=jnp.int32)
+    seen = (places[None, :] <= latent_offsets[:, None]).astype(jnp.bfloat16)
+    here = (places[None, :] == latent_offsets[:, None]).astype(jnp.bfloat16)
+    counts = jnp.dot(seen, token_hot, preferred_element_type=jnp.float32)
+    latent_hot = jnp.dot(here, token_hot, preferred_element_type=jnp.float32).astype(jnp.bfloat16)
+    key_table, value_table = (
+        jnp.dot(byte_table, w, preferred_element_type=jnp.float32).astype(jnp.bfloat16)
+        for w in (w_key, w_value)
+    )
+    latent_embed = jnp.dot(latent_hot, byte_table, preferred_element_type=jnp.float32).astype(
         jnp.bfloat16
     )
-    latent_embed = jnp.take(embedded, latent_offsets - hist_index * local_tokens, axis=0)
     latent_queries = jnp.dot(latent_embed, w_query, preferred_element_type=jnp.float32).astype(
         jnp.bfloat16
     )
-    pieces = (
-        lax.all_gather(hist_keys, "hist", axis=0, tiled=True),
-        lax.all_gather(hist_values, "hist", axis=0, tiled=True),
+    query_heads = latent_queries.reshape(latent_count, head_count, HEAD_DIM)
+    key_heads = key_table.reshape(vocab, head_count, HEAD_DIM)
+    value_heads = value_table.reshape(vocab, head_count, HEAD_DIM)
+    scores = jnp.einsum(
+        "qhd,khd->hqk", query_heads, key_heads, preferred_element_type=jnp.float32
+    ) * (1.0 / math.sqrt(HEAD_DIM))
+    present = counts[None] > 0.0
+    scores = jnp.where(present, scores, -1e30)
+    row_maxes = jnp.max(scores, axis=2, keepdims=True)
+    weights = jnp.where(present, jnp.exp(scores - row_maxes), 0.0) * counts[None]
+    totals = jnp.sum(weights, axis=2)
+    weighted = jnp.einsum(
+        "hqk,khd->hqd",
+        weights.astype(jnp.bfloat16),
+        value_heads,
+        preferred_element_type=jnp.float32,
     )
-    running = attend_block(
-        empty_state(latent_count, head_count),
-        latent_queries,
-        latent_offsets,
-        pieces[0],
-        pieces[1],
-        head_count,
-    )
-    cross_ctx = finish(running)
+    cross_ctx = finish((None, totals, weighted))
     partial_value = jnp.dot(cross_ctx, w_out, preferred_element_type=jnp.float32)
     shared_part = lax.psum_scatter(
         partial_value.astype(jnp.bfloat16), "mp", scatter_dimension=1, tiled=True

time: 603 us -> 399 us (0.66)
  the two profiles are of different devices: /device:TPU:1 before, /device:TPU:8 now
where the time goes in v1:
time: 399 us
  waiting for transfers between devices  214 us (54%)
  blocking collectives  143 us (36%)
  matrix products  22.5 us (6%)
  between operations  15.2 us (4%)
    reduce_scatter x1, waiting for transfers between devices, per_device(): lax.psum_scatter(partial_value.astype(jnp.bfloat16), 'mp', scatter_dimens...  87.6 us
    reduce_scatter x1, waiting for transfers between devices, per_device(): lax.psum_scatter(out_terms.astype(jnp.bfloat16), 'mp', scatter_dimension=...  80.8 us
    all_gather x1, blocking collectives, per_device(): latent_full = lax.all_gather(latent_part, 'mp', axis=1, tiled=True)  47.5 us
    all_gather x1, blocking collectives, per_device(): lax.all_gather(self_keys, 'hist', axis=0, tiled=True)  35 us
    all_gather x1, waiting for transfers between devices, per_device(): lax.all_gather(w_self_out, 'hist', axis=1, tiled=True)  34.8 us
    all_gather x1, blocking collectives, per_device(): all_ids = lax.all_gather(history_ids, 'hist', axis=0, tiled=True)  31.6 us
    all_gather x1, blocking collectives, per_device(): lax.all_gather(self_values, 'hist', axis=0, tiled=True)  29 us
    all_gather x1, waiting for transfers between devices, per_device(): lax.all_gather(w_self_value, 'hist', axis=0, tiled=True)  8.93 us
  transfers between devices with their start and end apart: 6, of which 4 were waited for; matrix products, arithmetic and copies ran while one was open for 2% of the time, Pallas kernels for 0%

profile of v1, /device:TPU:8, one launch (start us, length us, event | category | flops | bytes accessed | tf_op | source)
XLA Modules:
  0.0 398.8 jit_solution(745681493183731902)
XLA Ops:
  7.4 31.6 %all-gather = s32[16,1,512]{2,1,0:T(1,128)S(1)} all-gather(s32[1,1,512]{2,1,0:T(1,128)} %bitcast.81), channel_id=1, replica_groups=mesh['hist'=16,'mp'=16] {'hist'}, dimensions={0}, use_global_device_ids=true | all-gather | bytes 34816 | tf_op jit(solution)/shard_map/all_gather | solution.py:71
  39.0 2.5 broadcast_compare_fusion
  41.5 2.5 convolution_convert_fusion.2
  44.0 2.7 convolution_convert_fusion.4
  46.7 1.0 convolution_convert_fusion.3
  47.7 0.6 copy-done.2
  49.3 2.9 convolution_convert_fusion.1
  52.3 0.5 all-gather.6.cloned.1.call-update
  52.8 0.5 all-gather.8.cloned.1.call-update
  53.4 0.5 all-gather.10.cloned.1.call-update
  54.0 0.7 all-gather.12.cloned.1.call-update
  54.9 87.6 %reduce-scatter.3.cloned.1.call-done = bf16[64,256]{1,0:T(8,128)(2,1)} async-done(((bf16[64,4096]{1,0:T(8,128)(2,1)}), bf16[64,256]{1,0:T(8,128)(2,1)}) %reduce-scatter.3.cloned.1.call-update) | async-done | bytes 32784 | tf_op jit(solution)/shard_map/reduce_scatter | solution.py:109
  142.5 0.8 add_convert_fusion.1
  143.3 47.5 %all_gather.25 = bf16[64,4096]{1,0:T(8,128)(2,1)S(1)} all-gather(bf16[64,256]{1,0:T(8,128)(2,1)S(1)} %add_convert_fusion.1), channel_id=1, replica_groups=mesh['hist'=16,'mp'=16] {'mp'}, dimensions={1}, use_global_device_ids=true | all-gather | bytes 557056 | tf_op jit(solution)/shard_map/all_gather | solution.py:114
  191.0 2.2 fusion.19
  193.2 2.1 convolution_convert_fusion.6
  195.4 35.0 %all_gather.28 = bf16[1024,256]{1,0:T(8,128)(2,1)S(1)} all-gather(bf16[64,256]{1,0:T(8,128)(2,1)S(1)} %convolution_convert_fusion.6), channel_id=1, replica_groups=mesh['hist'=16,'mp'=16] {'hist'}, dimensions={0}, use_global_device_ids=true | all-gather | bytes 557056 | tf_op jit(solution)/shard_map/all_gather | solution.py:133
  231.0 8.9 %all-gather.10.cloned.1.call-done = bf16[4096,256]{1,0:T(8,128)(2,1)} async-done(((bf16[256,256]{1,0:T(8,128)(2,1)}), bf16[4096,256]{1,0:T(8,128)(2,1)}) %all-gather.10.cloned.1.call-update) | async-done | bytes 2097168 | tf_op jit(solution)/shard_map/all_gather | solution.py:123
  240.0 2.1 convolution_convert_fusion.5
  242.1 29.0 %all_gather.30 = bf16[1024,256]{1,0:T(8,128)(2,1)S(1)} all-gather(bf16[64,256]{1,0:T(8,128)(2,1)S(1)} %convolution_convert_fusion.5), channel_id=1, replica_groups=mesh['hist'=16,'mp'=16] {'hist'}, dimensions={0}, use_global_device_ids=true | all-gather | bytes 557056 | tf_op jit(solution)/shard_map/all_gather | solution.py:134
  271.4 34.8 %all-gather.12.cloned.1.call-done = bf16[256,4096]{1,0:T(8,128)(2,1)} async-done(((bf16[256,256]{1,0:T(8,128)(2,1)}), bf16[256,4096]{1,0:T(8,128)(2,1)}) %all-gather.12.cloned.1.call-update) | async-done | bytes 2097168 | tf_op jit(solution)/shard_map/all_gather | solution.py:147
  306.2 2.9 convolution_convert_fusion
  309.1 80.8 %reduce-scatter.5.cloned.1.call-done = bf16[64,256]{1,0:T(8,128)(2,1)} async-done(((bf16[64,4096]{1,0:T(8,128)(2,1)}), bf16[64,256]{1,0:T(8,128)(2,1)}) %reduce-scatter.5.cloned.1.call-update) | async-done | bytes 32784 | tf_op jit(solution)/shard_map/reduce_scatter | solution.py:150
  389.8 1.4 add_convert_fusion
  (31 shorter events, 2.6 us)
Async XLA Ops:
  7.4 34.1 %copy-start = (bf16[256,4096]{1,0:T(8,128)(2,1)S(1)}, bf16[256,4096]{1,0:T(8,128)(2,1)}, u32[]{:S(2)}) copy-start(bf16[256,4096]{1,0:T(8,128)(2,1)} %param.14) | copy-start | bytes 6291460
  7.4 34.1 %copy-start.4 = (s32[64]{0:T(128)S(1)}, s32[64]{0:T(128)}, u32[]{:S(2)}) copy-start(s32[64]{0:T(128)} %param.13) | copy-start | bytes 772
  7.4 135.1 %reduce-scatter.3.cloned.1.call-start = ((), (), s32[]{:S(2)}) async-start(), calls=%async_computation.2 | async-start | bytes 557056 | tf_op jit(solution)/shard_map/reduce_scatter | solution.py:109
  44.0 2.7 copy-start.1
  46.7 1.6 copy-start.2
  49.1 5.7 %copy-start.3 = (bf16[4096]{0:T(1024)(128)(2,1)S(1)}, bf16[4096]{0:T(1024)(128)(2,1)}, u32[]{:S(2)}) copy-start(bf16[4096]{0:T(1024)(128)(2,1)} %param.19) | copy-start | bytes 24580
  52.2 138.8 %all-gather.6.cloned.1.call-start = ((), (), s32[]{:S(2)}) async-start(), calls=%async_computation.3 | async-start | bytes 2228224 | tf_op jit(solution)/shard_map/all_gather | solution.py:121
  52.8 140.4 %all-gather.8.cloned.1.call-start = ((), (), s32[]{:S(2)}) async-start(), calls=%async_computation.4 | async-start | bytes 2228224 | tf_op jit(solution)/shard_map/all_gather | solution.py:122
  53.4 186.6 %all-gather.10.cloned.1.call-start = ((), (), s32[]{:S(2)}) async-start(), calls=%async_computation.5 | async-start | bytes 2228224 | tf_op jit(solution)/shard_map/all_gather | solution.py:123
  53.9 252.2 %all-gather.12.cloned.1.call-start = ((), (), s32[]{:S(2)}) async-start(), calls=%async_computation.6 | async-start | bytes 2228224 | tf_op jit(solution)/shard_map/all_gather | solution.py:147
  54.7 335.2 %reduce-scatter.5.cloned.1.call-start = ((), (), s32[]{:S(2)}) async-start(), calls=%async_computation.7 | async-start | bytes 557056 | tf_op jit(solution)/shard_map/reduce_scatter | solution.py:150
Sparse Core Ops, SparseCore 0:
  52.3 90.1 reduce-scatter.2
  309.2 80.5 reduce-scatter.4
Sparse Core Ops, SparseCore 1:
  55.7 57.7 all-gather.5
  116.4 61.8 all-gather.7
  181.1 58.8 all-gather.9
  242.9 63.3 all-gather.11

commit v2 on v0

v2 whole, which is shorter than its diff:
```python
import functools
import math

import jax
import jax.numpy as jnp
from jax import lax
from jax.experimental import pallas as pl
from jax.experimental.pallas import tpu as pltpu
from jax.sharding import PartitionSpec as P

HEAD_DIM = 128
MESH = pl.DeviceIdType.MESH
BF16 = jnp.bfloat16
F32 = jnp.float32
SCALE = 1.0 / math.sqrt(HEAD_DIM)
ROWS = 64
WIDE = 256
TOKENS = 512
NT = (((1,), (1,)), ((), ()))


def dot(a, b):
    return jnp.dot(a, b, preferred_element_type=F32)


def dot_nt(a, b):
    return lax.dot_general(a, b, NT, preferred_element_type=F32)


def kernel(
    small_ref, tab_hbm, wq_hbm, wk_hbm, wv_hbm, wo_hbm, wsq_hbm, wsk_hbm, wsv_hbm, wso_hbm,
    out_ref,
    ids, tab, wq, wk, wv, wo, wself, wso, ktab, qtab, vtab, acc, lat_hot,
    send1, recv1, mid, left, zsend, zrecv, ss_send, ss_recv, kv, queries, ctx, send2, recv2, resid,
    loc_sem, ids_s, ids_r, wself_s, wself_r, wso_s, wso_r, rs1_s, rs1_r, ag_s, ag_r,
    zx_s, zx_r, kv_s, kv_r, rs2_s, rs2_r, res_s, res_r,
):
    h = lax.axis_index("hist")
    m = lax.axis_index("mp")
    y, zh, c = h // 4, (h // 2) % 2, h % 2
    x, zl = m // 4, m % 4
    place = y * 2 + c

    def half_of(target_zl):
        own_pair = (target_zl // 2) == (zl // 2)
        inner = (zl == 1) | (zl == 2)
        return jnp.where(own_pair | inner, zh, 1 - zh)

    def peer(t):
        return (y * 4 + half_of(t % 4) * 2 + c, t)

    partner = (y * 4 + (1 - zh) * 2 + c, m)
    sibling = (y * 4 + zh * 2 + 1 - c, m)

    def y_peer(d):
        return (((y + d) % 4) * 4 + zh * 2 + c, m)

    def remote(src, dst, s, r, device):
        return pltpu.make_async_remote_copy(
            src_ref=src, dst_ref=dst, send_sem=s, recv_sem=r, device_id=device, device_id_type=MESH
        )

    def arrived(ref, sem):
        remote(ref, ref, sem, sem, partner).wait_recv()

    def left_here(ref, sem):
        remote(ref, ref, sem, sem, partner).wait_send()

    local = [
        pltpu.make_async_copy(small_ref.at[0:8], ids.at[h], loc_sem.at[0]),
        pltpu.make_async_copy(wsk_hbm, wself.at[place, 0], loc_sem.at[1]),
        pltpu.make_async_copy(wsv_hbm, wself.at[place, 1], loc_sem.at[2]),
        pltpu.make_async_copy(wsq_hbm, wself.at[place, 2], loc_sem.at[3]),
        pltpu.make_async_copy(wso_hbm, wso.at[h], loc_sem.at[4]),
        pltpu.make_async_copy(tab_hbm, tab, loc_sem.at[5]),
        pltpu.make_async_copy(wk_hbm, wk, loc_sem.at[6]),
        pltpu.make_async_copy(wv_hbm, wv, loc_sem.at[7]),
        pltpu.make_async_copy(wq_hbm, wq, loc_sem.at[8]),
    ]
    for b in range(8):
        column = ((b // 2) * 4 + half_of(b % 4) * 2 + (b % 2)) * WIDE
        local.append(
            pltpu.make_async_copy(
                wo_hbm.at[:, pl.ds(pl.multiple_of(column, WIDE), WIDE)], wo.at[b], loc_sem.at[9 + b]
            )
        )
    for copy in local:
        copy.start()

    barrier = pltpu.get_barrier_semaphore()

    @pl.loop(1, 32)
    def _(i):
        other = (zh * 16 + m + i) % 32
        device = (y * 4 + (other // 16) * 2 + c, other % 16)
        pl.semaphore_signal(barrier, inc=1, device_id=device, device_id_type=MESH)

    @pl.loop(1, 16)
    def _(i):
        pl.semaphore_signal(barrier, inc=1, device_id=((h + i) % 16, m), device_id_type=MESH)

    pl.semaphore_wait(barrier, 46)

    local[0].wait()

    @pl.loop(1, 16)
    def _(i):
        remote(ids.at[h], ids.at[h], ids_s.at[i], ids_r.at[h], ((h + i) % 16, m)).start()

    for copy in local[1:5]:
        copy.wait()
    for d in (1, 3, 2):
        remote(
            wself.at[place], wself.at[place], wself_s.at[d], wself_r.at[place], y_peer(d)
        ).start()
    remote(wself.at[place], wself.at[place], wself_s.at[0], wself_r.at[place], sibling).start()
    remote(wso.at[h], wso.at[h], wso_s.at[0], wso_r.at[h], partner).start()

    local[5].wait()
    local[6].wait()
    ktab[...] = dot(tab[...], wk[...]).astype(BF16)
    local[7].wait()
    vtab[...] = dot(tab[...], wv[...]).astype(BF16)
    local[8].wait()
    qtab[...] = dot(tab[...], wq[...]).astype(BF16)

    @pl.loop(1, 16)
    def _(i):
        b = (h + i) % 16
        arrived(ids.at[b], ids_r.at[b])

    offsets = ids[y * 4 + c][4:5, :] + ids[y * 4 + 2 + c][5:6, :]
    acc[...] = jnp.zeros_like(acc)
    vocab_iota = lax.broadcasted_iota(jnp.int32, (256, 128), 0).astype(F32)
    row_iota = lax.broadcasted_iota(jnp.int32, (128, 128), 0)

    @pl.loop(0, 16)
    def _(b):
        hots, masks = [], []
        for r in range(4):
            hots.append(jnp.where(vocab_iota == ids[b, r : r + 1, :], 1.0, 0.0).astype(BF16))
            places = (row_iota + (b * TOKENS + r * 128)).astype(F32)
            masks.append(
                jnp.concatenate(
                    [
                        jnp.where(places <= offsets, 1.0, 0.0).astype(BF16),
                        jnp.where(places == offsets, 1.0, 0.0).astype(BF16),
                    ],
                    axis=1,
                )
            )
        acc[...] += dot(jnp.concatenate(hots, axis=1), jnp.concatenate(masks, axis=0))

    counts = acc[:, :128].T
    hot = acc[:, 128:].T.astype(BF16)
    lat_hot[...] = hot
    latent_queries = dot(hot, qtab[...]).astype(BF16)
    present = counts > 0.0
    heads = []
    for hd in range(2):
        cols = slice(hd * HEAD_DIM, (hd + 1) * HEAD_DIM)
        scores = dot_nt(latent_queries[:, cols], ktab[:, cols]) * SCALE
        scores = jnp.where(present, scores, -1e30)
        top = jnp.max(scores, axis=1, keepdims=True)
        weights = jnp.where(present, jnp.exp(scores - top), 0.0) * counts
        total = jnp.sum(weights, axis=1, keepdims=True)
        heads.append(dot(weights.astype(BF16), vtab[:, cols]) / total)
    ctx[...] = jnp.concatenate(heads, axis=1).astype(BF16)

    for copy in local[9:]:
        copy.wait()

    @pl.loop(0, 8)
    def _(i):
        b = (m + i) % 8
        part = dot(ctx[...], wo[b]).astype(BF16)
        for r in range(2):
            t = r * 8 + b
            block = part[r * ROWS : (r + 1) * ROWS]
            send1[t] = block

            @pl.when(t == m)
            def _():
                recv1[m] = block

            @pl.when(t != m)
            def _():
                remote(send1.at[t], recv1.at[m], rs1_s.at[t], rs1_r.at[m], peer(t)).start()

    own_block = ((m % 8) // 2) * 4 + zh * 2 + m % 2
    total = dot(
        lat_hot[pl.ds(pl.multiple_of((m // 8) * ROWS, ROWS), ROWS)],
        tab[:, pl.ds(pl.multiple_of(own_block * WIDE, WIDE), WIDE)],
    )

    @pl.loop(1, 16)
    def _(i):
        s = (m + i) % 16
        arrived(recv1.at[s], rs1_r.at[s])

    sums = recv1[0].astype(F32)
    for s in range(1, 16):
        sums += recv1[s].astype(F32)
    mid[m] = (total + sums).astype(BF16)

    for d in range(1, 4):
        remote(
            mid.at[m], mid.at[m], ag_s.at[d], ag_r.at[m], (h, x * 4 + (zl + d) % 4)
        ).start()
    for d in (1, 3, 2):
        remote(
            mid.at[m], mid.at[m], ag_s.at[4 + d], ag_r.at[m], (h, ((x + d) % 4) * 4 + zl)
        ).start()
    for e in range(1, 4):
        t = x * 4 + (zl + e) % 4
        arrived(mid.at[t], ag_r.at[t])
        for d in (1, 3, 2):
            remote(
                mid.at[t], mid.at[t], ag_s.at[4 + e * 4 + d], ag_r.at[t], (h, ((x + d) % 4) * 4 + zl)
            ).start()

    for d in (1, 3, 2):
        slot = ((y + d) % 4) * 2 + c
        arrived(wself.at[slot], wself_r.at[slot])
        remote(
            wself.at[slot], wself.at[slot], wself_s.at[4 + d], wself_r.at[slot], sibling
        ).start()
    far = y * 4 + (1 - zh) * 2 + c
    arrived(wso.at[far], wso_r.at[far])
    for d in (1, 3, 2):
        remote(wso.at[h], wso.at[h], wso_s.at[d], wso_r.at[h], y_peer(d)).start()
        remote(wso.at[far], wso.at[far], wso_s.at[4 + d], wso_r.at[far], y_peer(d)).start()

    @pl.loop(4, 16)
    def _(i):
        t = (m - m % 4 + i) % 16
        arrived(mid.at[t], ag_r.at[t])

    squares = jnp.zeros((128, 128), F32)
    for b in range(8):
        rows = jnp.concatenate([mid[b], mid[8 + b]], axis=0).astype(F32)
        squares += rows[:, :128] * rows[:, :128] + rows[:, 128:] * rows[:, 128:]
        gain_row = 8 + ((b // 2) * 4 + zh * 2 + b % 2) * 2
        gain = jnp.concatenate(
            [small_ref[pl.ds(gain_row, 1), :], small_ref[pl.ds(gain_row + 1, 1), :]], axis=1
        )
        left[b] = (rows * gain).astype(BF16)
    square = jnp.broadcast_to(jnp.sum(squares, axis=1, keepdims=True), (128, 128)).T
    ss_send[...] = square[0:8]
    remote(ss_send, ss_recv, zx_s.at[3], zx_r.at[3], partner).start()

    for d in range(4):
        slot = d * 2 + 1 - c
        arrived(wself.at[slot], wself_r.at[slot])
    parts = []
    for j in range(3):
        part = dot(left[0], wself[0, j])
        for b in range(1, 8):
            part += dot(left[b], wself[b, j])
        parts.append(part)
        zsend[j] = part.astype(BF16)
        remote(zsend.at[j], zrecv.at[j], zx_s.at[j], zx_r.at[j], partner).start()

    own_bit = (m // 2) % 2
    home = (m // 4) * 2 + m % 2

    @pl.when(own_bit == zh)
    def _():
        away = (1 - zh) * 8 + home
        remote(mid.at[away], resid, res_s.at[0], res_r.at[0], partner).start()
        resid[...] = mid[zh * 8 + home]

    arrived(ss_recv, zx_r.at[3])
    square = ss_send[0:1] + ss_recv[0:1]
    norm = lax.rsqrt(square * (1.0 / 4096.0) + 1e-05)
    norm = jnp.broadcast_to(norm, (128, 128)).T
    norm = jnp.concatenate([norm, norm], axis=1)

    own_rows = pl.ds(pl.multiple_of(place * 128, 128), 128)
    for j in range(2):
        arrived(zrecv.at[j], zx_r.at[j])
        kv[j, own_rows, :] = ((parts[j] + zrecv[j].astype(F32)) * norm).astype(BF16)
        block = kv.at[j, own_rows, :]
        for d in (1, 3, 2):
            remote(block, block, kv_s.at[j * 8 + d], kv_r.at[j * 8 + place], y_peer(d)).start()
        remote(block, block, kv_s.at[j * 8], kv_r.at[j * 8 + place], sibling).start()
    arrived(zrecv.at[2], zx_r.at[2])
    queries[...] = ((parts[2] + zrecv[2].astype(F32)) * norm).astype(BF16)

    def kv_block(j, slot):
        return kv.at[j, pl.ds(pl.multiple_of(slot * 128, 128), 128), :]

    for j in range(2):
        for d in (1, 3, 2):
            slot = ((y + d) % 4) * 2 + c
            block = kv_block(j, slot)
            arrived(block, kv_r.at[j * 8 + slot])
            remote(block, block, kv_s.at[j * 8 + 4 + d], kv_r.at[j * 8 + slot], sibling).start()

    for d in (1, 3, 2):
        for half in range(2):
            slot = ((y + d) % 4) * 4 + half * 2 + c
            arrived(wso.at[slot], wso_r.at[slot])
    for d in range(4):
        for half in range(2):
            slot = d * 4 + half * 2 + c
            remote(
                wso.at[slot], wso.at[slot], wso_s.at[8 + d * 2 + half], wso_r.at[slot], sibling
            ).start()

    for j in range(2):
        for d in range(4):
            slot = d * 2 + 1 - c
            arrived(kv_block(j, slot), kv_r.at[j * 8 + slot])

    key_lane = lax.broadcasted_iota(jnp.int32, (128, 1024), 1)
    key_in = key_lane % 128
    key_place = (
        (key_lane // 256) * 256 + ((key_lane // 128) % 2) * 64 + (key_in // 64) * 128 + key_in % 64
    )
    query_row = lax.broadcasted_iota(jnp.int32, (128, 1024), 0)
    query_place = y * 256 + c * 64 + (query_row // 64) * 128 + query_row % 64
    allowed = key_place <= query_place
    heads = []
    for hd in range(2):
        cols = slice(hd * HEAD_DIM, (hd + 1) * HEAD_DIM)
        scores = dot_nt(queries[:, cols], kv[0, :, cols]) * SCALE
        scores = jnp.where(allowed, scores, -1e30)
        top = jnp.max(scores, axis=1, keepdims=True)
        weights = jnp.where(allowed, jnp.exp(scores - top), 0.0)
        total = jnp.sum(weights, axis=1, keepdims=True)
        heads.append(dot(weights.astype(BF16), kv[1, :, cols]) / total)
    ctx[...] = jnp.concatenate(heads, axis=1).astype(BF16)

    for d in range(4):
        for half in range(2):
            slot = d * 4 + half * 2 + 1 - c
            arrived(wso.at[slot], wso_r.at[slot])

    @pl.loop(0, 16)
    def _(i):
        t = (m + i) % 16
        rows = pl.ds(pl.multiple_of(half_of(t % 4) * ROWS, ROWS), ROWS)
        send2[t] = dot(ctx[rows, :], wso[t]).astype(BF16)

        @pl.when(t == m)
        def _():
            recv2[m] = send2[m]

        @pl.when(t != m)
        def _():
            remote(send2.at[t], recv2.at[m], rs2_s.at[t], rs2_r.at[m], peer(t)).start()

    @pl.when(own_bit != zh)
    def _():
        arrived(resid, res_r.at[0])

    @pl.loop(1, 16)
    def _(i):
        s = (m + i) % 16
        arrived(recv2.at[s], rs2_r.at[s])

    sums = resid[...].astype(F32)
    for s in range(16):
        sums += recv2[s].astype(F32)
    out_ref[...] = sums.astype(BF16)

    @pl.loop(1, 16)
    def _(i):
        left_here(ids.at[h], ids_s.at[i])
        s = (m + i) % 16
        left_here(send1.at[s], rs1_s.at[s])
        left_here(send2.at[s], rs2_s.at[s])

    @pl.loop(0, 8)
    def _(i):
        @pl.when(i != 4)
        def _():
            left_here(wself.at[0], wself_s.at[i])
            left_here(kv_block(0, 0), kv_s.at[i])
            left_here(kv_block(0, 0), kv_s.at[8 + i])

    @pl.loop(0, 16)
    def _(i):
        @pl.when(i != 4)
        def _():
            left_here(wso.at[0], wso_s.at[i])

    for i in (1, 2, 3, 5, 6, 7, 9, 10, 11, 13, 14, 15, 17, 18, 19):
        left_here(mid.at[0], ag_s.at[i])
    for j in range(3):
        left_here(zsend.at[j], zx_s.at[j])
    left_here(ss_send, zx_s.at[3])

    @pl.when(own_bit == zh)
    def _():
        left_here(resid, res_s.at[0])


def per_device(
    history_ids, latent_offsets, byte_table, w_query, w_key, w_value, w_out, norm_gain,
    w_self_query, w_self_key, w_self_value, w_self_out,
):
    offsets = latent_offsets.astype(F32)
    small = jnp.concatenate(
        [
            history_ids.astype(F32),
            offsets,
            jnp.zeros((128,), F32),
            offsets,
            jnp.zeros((256,), F32),
            norm_gain.astype(F32),
        ]
    ).reshape(40, 128)
    vmem = pl.BlockSpec(memory_space=pltpu.VMEM)
    hbm = pl.BlockSpec(memory_space=pl.ANY)
    dma = pltpu.SemaphoreType.DMA
    scratch = [
        pltpu.VMEM((16, 8, 128), F32),
        pltpu.VMEM((256, 4096), BF16),
        pltpu.VMEM((4096, 256), BF16),
        pltpu.VMEM((4096, 256), BF16),
        pltpu.VMEM((4096, 256), BF16),
        pltpu.VMEM((8, 256, 256), BF16),
        pltpu.VMEM((8, 3, 256, 256), BF16),
        pltpu.VMEM((16, 256, 256), BF16),
        pltpu.VMEM((256, 256), BF16),
        pltpu.VMEM((256, 256), BF16),
        pltpu.VMEM((256, 256), BF16),
        pltpu.VMEM((256, 256), F32),
        pltpu.VMEM((128, 256), BF16),
        pltpu.VMEM((16, ROWS, WIDE), BF16),
        pltpu.VMEM((16, ROWS, WIDE), BF16),
        pltpu.VMEM((16, ROWS, WIDE), BF16),
        pltpu.VMEM((8, 128, WIDE), BF16),
        pltpu.VMEM((3, 128, WIDE), BF16),
        pltpu.VMEM((3, 128, WIDE), BF16),
        pltpu.VMEM((8, 128), F32),
        pltpu.VMEM((8, 128), F32),
        pltpu.VMEM((2, 1024, WIDE), BF16),
        pltpu.VMEM((128, WIDE), BF16),
        pltpu.VMEM((128, WIDE), BF16),
        pltpu.VMEM((16, ROWS, WIDE), BF16),
        pltpu.VMEM((16, ROWS, WIDE), BF16),
        pltpu.VMEM((ROWS, WIDE), BF16),
    ] + [dma((n,)) for n in (17, 16, 16, 8, 8, 16, 16, 16, 16, 20, 16, 4, 4, 16, 16, 16, 16, 1, 1)]
    return pl.pallas_call(
        kernel,
        out_shape=jax.ShapeDtypeStruct((ROWS, WIDE), BF16),
        in_specs=[vmem] + [hbm] * 9,
        out_specs=vmem,
        scratch_shapes=scratch,
        compiler_params=pltpu.CompilerParams(
            collective_id=0, has_side_effects=True, vmem_limit_bytes=56 * 1024 * 1024
        ),
        cost_estimate=pl.CostEstimate(
            flops=5_000_000_000, bytes_accessed=12_000_000, transcendentals=400_000
        ),
    )(
        small, byte_table, w_query, w_key, w_value, w_out,
        w_self_query, w_self_key, w_self_value, w_self_out,
    )


def solution(mesh):
    return jax.shard_map(
        per_device,
        mesh=mesh,
        in_specs=(
            P("hist"),
            P("hist"),
            P(),
            P(None, "mp"),
            P(None, "mp"),
            P(None, "mp"),
            P("mp", None),
            P(),
            P("hist", "mp"),
            P("hist", "mp"),
            P("hist", "mp"),
            P("mp", "hist"),
        ),
        out_specs=P("hist", "mp"),
        check_vma=False,
    )
```

time: 603 us -> 77 us (0.13); the launches traced: 592 us -> 76.7 us
  waiting for transfers between devices: 435 us -> 0 us
  blocking collectives: 94 us -> 0 us
  Pallas kernels: 0 us -> 72.6 us
  matrix products: 28.7 us -> 0 us
  between operations: 13.7 us -> 0.01 us
  local copies, waits for them, and re-layouts: 12.5 us -> 2.75 us
  other arithmetic: 8.74 us -> 1.34 us
    all_gather x6 -> x0, waiting for transfers between devices: 298 us -> none  [the longest x1 70 us: per_device(): lax.all_gather(hist_keys, 'hist', axis=0, tiled=True)]
    reduce_scatter x2 -> x0, waiting for transfers between devices: 134 us -> none  [the longest x1 68.8 us: per_device(): lax.psum_scatter(out_terms.astype(jnp.bfloat16), 'mp', scatter_dimension=...]
    all_gather x3 -> x0, blocking collectives: 94 us -> none  [the longest x1 36.8 us: per_device(): latent_full = lax.all_gather(latent_part, 'mp', axis=1, tiled=True)]
    pallas_call x0 -> x1, Pallas kernels: none -> 72.6 us  [per_device(): pl.pallas_call(kernel, out_shape=jax.ShapeDtypeStruct((ROWS, WIDE), BF16)...]
    dot_general x12 -> x0, matrix products: 28.7 us -> none  [the longest x3 6.33 us: per_device(): jnp.dot(normed, piece, preferred_element_type=jnp.float32)]
    gather x2 -> x0, local copies, waits for them, and re-layouts: 8.46 us -> none  [the longest x1 4.36 us: per_device(): embedded = jnp.take(byte_table, history_ids, axis=0)]
  transfers between devices with their start and end apart: 8 -> 0, of which waited for: 8 -> 0; matrix products, arithmetic and copies ran while one was open for 4% -> 0% of each run, Pallas kernels for 0% -> 0%
where the time goes in v2:
time: 77 us; the launch traced here: 76.7 us
  Pallas kernels  72.6 us (94%)
  local copies, waits for them, and re-layouts  2.75 us (4%)
  other arithmetic  1.34 us (2%)
    pallas_call x1, Pallas kernels, per_device(): pl.pallas_call(kernel, out_shape=jax.ShapeDtypeStruct((ROWS, WIDE), BF16)...  72.6 us

profile of v2, /device:TPU:1, one launch (start us, length us, event | category | flops | bytes accessed | tf_op | source)
XLA Modules:
  0.0 76.7 jit_solution(3941541385166044254)
XLA Ops:
  0.0 0.7 convert_element_type.10
  0.7 0.7 convert_element_type.9
  1.3 1.4 %concatenate.3 = f32[5120]{0:T(1024)} concatenate(f32[512]{0:T(512)S(1)} %convert_element_type.9, f32[64]{0:T(128)S(1)} %convert_element_type.10, f32[128]{0:T(128)S(1)} %broadcast_in_dim.6, f32[64]{0:T(128)S(1)} %convert_element_type.10, f32[256]{0:T(256)S(1)} %broadcast_in_dim.7, bf16[4096]{0:T(1024)(128)(2,1)} %param.19), dimensions={0} | concatenate | bytes 32768 | tf_op jit(solution)/shard_map/concatenate | solution.py:405
  2.7 72.6 %shard_map.118 = bf16[64,256]{1,0:T(8,128)(2,1)} custom-call(f32[40,128]{1,0:T(8,128)} %bitcast.1, bf16[256,4096]{1,0:T(8,128)(2,1)} %tab_hbm.1, bf16[4096,256]{1,0:T(8,128)(2,1)} %wq_hbm.1, bf16[4096,256]{1,0:T(8,128)(2,1)} %wk_hbm.1, bf16[4096,256]{1,0:T(8,128)(2,1)} %wv_hbm.1, bf16[256,4096]{1,0:T(8,128)(2,1)} %wo_hbm.1, bf16[256,256]{1,0:T(8,128)(2,1)} %wsq_hbm.1, ...), custom_call_target="tpu_custom_call" | custom-call | flops 5000000000 | bytes 12000000 | tf_op jit(solution)/shard_map/pallas_call | solution.py:447
  75.3 1.4 %copy.14 = bf16[64,256]{1,0:T(8,128)(2,1)} copy(bf16[64,256]{1,0:T(8,128)(2,1)} %shard_map.118) | data formatting | bytes 65536
  (2 shorter events, 0.0 us)

commit v3 on v2

v3 whole, which is shorter than its diff:
```python
import functools
import math

import jax
import jax.numpy as jnp
from jax import lax
from jax.experimental import pallas as pl
from jax.experimental.pallas import tpu as pltpu
from jax.sharding import PartitionSpec as P

HEAD_DIM = 128
MESH = pl.DeviceIdType.MESH
BF16 = jnp.bfloat16
F32 = jnp.float32
SCALE = 1.0 / math.sqrt(HEAD_DIM)
ROWS = 64
WIDE = 256
TOKENS = 512
NT = (((1,), (1,)), ((), ()))


def dot(a, b):
    return jnp.dot(a, b, preferred_element_type=F32)


def dot_nt(a, b):
    return lax.dot_general(a, b, NT, preferred_element_type=F32)


def kernel(
    ids_hbm, offs_hbm, gain_hbm, tab_hbm, wq_hbm, wk_hbm, wv_hbm, wo_hbm,
    wsq_hbm, wsk_hbm, wsv_hbm, wso_hbm,
    out_ref,
    ids, offs, gains, gain_rows, tab, wq, wk, wv, wo, wself, wso, ktab, qtab, vtab, lat_hot,
    send1, recv1, mid, left, zsend, zrecv, ss_send, ss_recv, kv, queries, ctx, send2, recv2, resid,
    loc_sem, ids_s, ids_r, wself_s, wself_r, wso_s, wso_r, rs1_s, rs1_r, ag_s, ag_r,
    zx_s, zx_r, kv_s, kv_r, rs2_s, rs2_r, res_s, res_r, offs_s, offs_r,
):
    h = lax.axis_index("hist")
    m = lax.axis_index("mp")
    y, zh, c = h // 4, (h // 2) % 2, h % 2
    x, zl = m // 4, m % 4
    place = y * 2 + c
    at_edge = (zl == 0) | (zl == 3)
    nearest = jnp.where(zl < 2, 3, 0)
    served = jnp.where(zl == 0, 2, 0)

    def half_of(target_zl):
        own_pair = (target_zl // 2) == (zl // 2)
        inner = (zl == 1) | (zl == 2)
        return jnp.where(own_pair | inner, zh, 1 - zh)

    def peer(t):
        return (y * 4 + half_of(t % 4) * 2 + c, t)

    def source(t):
        return (y * 4 + jnp.where(t % 4 == nearest, 1 - zh, zh) * 2 + c, t)

    partner = (y * 4 + (1 - zh) * 2 + c, m)
    sibling = (y * 4 + zh * 2 + 1 - c, m)

    def same_z(i):
        other = (place + i) % 8
        return ((other // 2) * 4 + zh * 2 + other % 2, m)

    def y_peer(d):
        return (((y + d) % 4) * 4 + zh * 2 + c, m)

    def remote(src, dst, s, r, device):
        return pltpu.make_async_remote_copy(
            src_ref=src, dst_ref=dst, send_sem=s, recv_sem=r, device_id=device, device_id_type=MESH
        )

    def arrived(ref, sem):
        remote(ref, ref, sem, sem, partner).wait_recv()

    def left_here(ref, sem):
        remote(ref, ref, sem, sem, partner).wait_send()

    far = y * 4 + (1 - zh) * 2 + c

    def half_slot(slot, k):
        return wso.at[slot, pl.ds(k * 128, 128)]

    def cross_output_weights(k):
        part = half_slot(h, k)
        remote(part, part, wso_s.at[k], wso_r.at[16 + h * 2 + k], partner).start()

    def spread_far(k):
        part = half_slot(far, k)
        arrived(part, wso_r.at[16 + far * 2 + k])
        for d in (1, 3, 2):
            remote(
                part, part, wso_s.at[6 + k * 4 + d], wso_r.at[16 + far * 2 + k], y_peer(d)
            ).start()

    barrier = pltpu.get_barrier_semaphore()

    def greet(device):
        pl.semaphore_signal(barrier, inc=1, device_id=device, device_id_type=MESH)

    greet(partner)

    @pl.loop(0, 8)
    def _(i):
        greet(((i // 2) * 4 + (1 - zh) * 2 + i % 2, x * 4 + nearest))

    @pl.loop(1, 16)
    def _(i):
        t = (m + i) % 16
        greet(source(t))

    @pl.loop(1, 8)
    def _(i):
        greet(same_z(i))

    @pl.loop(1, 4)
    def _(i):
        greet((h, x * 4 + (zl + i) % 4))

    local = [
        pltpu.make_async_copy(ids_hbm, ids.at[h], loc_sem.at[0]),
        pltpu.make_async_copy(offs_hbm, offs.at[zh], loc_sem.at[17]),
        pltpu.make_async_copy(wsk_hbm, wself.at[place, 0], loc_sem.at[1]),
        pltpu.make_async_copy(wsv_hbm, wself.at[place, 1], loc_sem.at[2]),
        pltpu.make_async_copy(wsq_hbm, wself.at[place, 2], loc_sem.at[3]),
        pltpu.make_async_copy(wso_hbm, wso.at[h], loc_sem.at[4]),
        pltpu.make_async_copy(tab_hbm, tab, loc_sem.at[5]),
        pltpu.make_async_copy(wk_hbm, wk, loc_sem.at[6]),
        pltpu.make_async_copy(wv_hbm, wv, loc_sem.at[7]),
        pltpu.make_async_copy(wq_hbm, wq, loc_sem.at[8]),
        pltpu.make_async_copy(gain_hbm, gains, loc_sem.at[18]),
    ]
    for b in range(8):
        column = ((b // 2) * 4 + half_of(b % 4) * 2 + (b % 2)) * WIDE
        local.append(
            pltpu.make_async_copy(
                wo_hbm.at[:, pl.ds(pl.multiple_of(column, WIDE), WIDE)], wo.at[b], loc_sem.at[9 + b]
            )
        )
    for copy in local:
        copy.start()

    pl.semaphore_wait(barrier, 26 + jnp.where(at_edge, 16, 0))

    @pl.when(at_edge)
    def _():
        @pl.loop(0, 16)
        def _(i):
            device = (((i // 2) % 4) * 4 + (1 - zh) * 2 + i % 2, x * 4 + served + i // 8)
            remote(ids_hbm, ids.at[h], ids_s.at[8 + i], ids_r.at[h], device).start()

        for i in range(2):
            device = (y * 4 + (1 - zh) * 2 + c, x * 4 + served + i)
            remote(offs_hbm, offs.at[zh], offs_s.at[i], offs_r.at[0], device).start()

    @pl.loop(1, 8)
    def _(i):
        remote(ids_hbm, ids.at[h], ids_s.at[i], ids_r.at[h], same_z(i)).start()

    for copy in local[2:6]:
        copy.wait()
    for d in (1, 3, 2):
        remote(
            wself.at[place], wself.at[place], wself_s.at[d], wself_r.at[place], y_peer(d)
        ).start()
    remote(wself.at[place], wself.at[place], wself_s.at[0], wself_r.at[place], sibling).start()

    local[6].wait()
    local[7].wait()
    ktab[...] = dot(tab[...], wk[...]).astype(BF16)
    local[8].wait()
    vtab[...] = dot(tab[...], wv[...]).astype(BF16)
    local[9].wait()
    qtab[...] = dot(tab[...], wq[...]).astype(BF16)

    local[0].wait()
    local[1].wait()

    @pl.loop(1, 8)
    def _(i):
        other = (place + i) % 8
        b = (other // 2) * 4 + zh * 2 + other % 2
        arrived(ids.at[b], ids_r.at[b])

    vocab_iota = lax.broadcasted_iota(jnp.int32, (256, 128), 0)
    row_iota = lax.broadcasted_iota(jnp.int32, (128, 128), 0)

    def earlier(half, seen):
        def add(i, seen):
            b = (i // 2) * 4 + half * 2 + i % 2
            return sum(
                (jnp.where(vocab_iota == ids[b, r : r + 1, :], 1.0, 0.0) for r in range(4)), seen
            )

        return lax.fori_loop(0, y * 2, add, seen)

    def token_hot(b):
        return jnp.concatenate(
            [jnp.where(vocab_iota == ids[b, r : r + 1, :], 1.0, 0.0).astype(BF16) for r in range(4)],
            axis=1,
        )

    def masks(b, offsets):
        blocks = []
        for r in range(4):
            places = row_iota + (b * TOKENS + r * 128)
            blocks.append(
                jnp.concatenate(
                    [
                        jnp.where(places <= offsets, 1.0, 0.0).astype(BF16),
                        jnp.where(places == offsets, 1.0, 0.0).astype(BF16),
                    ],
                    axis=1,
                )
            )
        return jnp.concatenate(blocks, axis=0)

    seen = earlier(zh, jnp.zeros((256, 128), F32))
    near_hots = [token_hot(y * 4 + zh * 2 + q) for q in range(2)]

    @pl.loop(0, 8)
    def _(i):
        b = (i // 2) * 4 + (1 - zh) * 2 + i % 2
        arrived(ids.at[b], ids_r.at[b])

    arrived(offs.at[1 - zh], offs_r.at[0])

    cross_output_weights(0)

    offsets = jnp.concatenate([offs[0], offs[1]], axis=1)
    counted = jnp.zeros((256, 256), F32)
    for q in range(2):
        counted += dot(near_hots[q], masks(y * 4 + zh * 2 + q, offsets))
        b = y * 4 + (1 - zh) * 2 + q
        counted += dot(token_hot(b), masks(b, offsets))
    seen = earlier(1 - zh, seen)

    counts = (counted[:, :128] + jnp.sum(seen, axis=1, keepdims=True)).T
    hot = counted[:, 128:].T.astype(BF16)
    lat_hot[...] = hot
    latent_queries = dot(hot, qtab[...]).astype(BF16)
    present = counts > 0.0
    heads = []
    for hd in range(2):
        cols = slice(hd * HEAD_DIM, (hd + 1) * HEAD_DIM)
        scores = dot_nt(latent_queries[:, cols], ktab[:, cols]) * SCALE
        scores = jnp.where(present, scores, -1e30)
        top = jnp.max(scores, axis=1, keepdims=True)
        weights = jnp.where(present, jnp.exp(scores - top), 0.0) * counts
        total = jnp.sum(weights, axis=1, keepdims=True)
        heads.append(dot(weights.astype(BF16), vtab[:, cols]) / total)
    ctx[...] = jnp.concatenate(heads, axis=1).astype(BF16)

    for copy in local[11:]:
        copy.wait()
    turn = 3 - 2 * (zl % 2)
    z_order = [(zl + e) % 4 for e in (2, turn, 4 - turn, 0)]
    for other in z_order:
        for e in range(2):
            b = ((x + e) % 2) * 4 + other
            part = dot(ctx[...], wo[b]).astype(BF16)
            send1[b] = part[:ROWS]
            send1[8 + b] = part[ROWS:]
            for d in (1, 3) if e else (2, 0):
                t = ((x + d) % 4) * 4 + other

                def send(t=t):
                    remote(send1.at[t], recv1.at[m], rs1_s.at[t], rs1_r.at[m], peer(t)).start()

                if d or other is not z_order[3]:
                    send()
    recv1[m] = send1[m]

    own_block = ((m % 8) // 2) * 4 + zh * 2 + m % 2
    total = dot(
        lat_hot[pl.ds(pl.multiple_of((m // 8) * ROWS, ROWS), ROWS)],
        tab[:, pl.ds(pl.multiple_of(own_block * WIDE, WIDE), WIDE)],
    )

    @pl.loop(1, 16)
    def _(i):
        s = (m + i) % 16
        arrived(recv1.at[s], rs1_r.at[s])

    sums = recv1[0].astype(F32)
    for s in range(1, 16):
        sums += recv1[s].astype(F32)
    mid[m] = (total + sums).astype(BF16)

    order = (zl + 1 - 2 * (zl % 2), jnp.where(zl < 2, 2, 1), jnp.where(zl < 2, 3, 0))
    for e, other in enumerate(order):
        remote(
            mid.at[m], mid.at[m], ag_s.at[1 + e], ag_r.at[m], (h, x * 4 + other)
        ).start()
    for d in (1, 3, 2):
        remote(
            mid.at[m], mid.at[m], ag_s.at[4 + d], ag_r.at[m], (h, ((x + d) % 4) * 4 + zl)
        ).start()
    for d in (1, 3, 2):
        remote(wso.at[h], wso.at[h], wso_s.at[2 + d], wso_r.at[h], y_peer(d)).start()
    spread_far(0)

    for e, other in enumerate(order):
        t = x * 4 + other
        arrived(mid.at[t], ag_r.at[t])
        for d in (1, 3, 2):
            remote(
                mid.at[t], mid.at[t], ag_s.at[8 + e * 4 + d], ag_r.at[t], (h, ((x + d) % 4) * 4 + zl)
            ).start()

    cross_output_weights(1)

    for d in (1, 3, 2):
        slot = ((y + d) % 4) * 2 + c
        arrived(wself.at[slot], wself_r.at[slot])
        remote(
            wself.at[slot], wself.at[slot], wself_s.at[4 + d], wself_r.at[slot], sibling
        ).start()

    local[10].wait()
    gain_rows[...] = gains[...].astype(F32)

    @pl.loop(4, 16)
    def _(i):
        t = (m - m % 4 + i) % 16
        arrived(mid.at[t], ag_r.at[t])

    squares = jnp.zeros((128, 128), F32)
    for b in range(8):
        rows = jnp.concatenate([mid[b], mid[8 + b]], axis=0).astype(F32)
        squares += rows[:, :128] * rows[:, :128] + rows[:, 128:] * rows[:, 128:]
        first = ((b // 2) * 4 + zh * 2 + b % 2) * 2
        gain = [gain_rows[pl.ds(first + i, 1), :] for i in range(2)]
        left[b] = (rows * jnp.concatenate(gain, axis=1)).astype(BF16)

    for d in range(4):
        slot = d * 2 + 1 - c
        arrived(wself.at[slot], wself_r.at[slot])

    def project(j):
        part = dot(left[0], wself[0, j])
        for b in range(1, 8):
            part += dot(left[b], wself[b, j])
        zsend[j, 0] = part[:ROWS].astype(BF16)
        zsend[j, 1] = part[ROWS:].astype(BF16)
        return part

    def push(j):
        for r in range(2):
            k = j * 2 + r
            remote(zsend.at[j, r], zrecv.at[j, r], zx_s.at[k], zx_r.at[k], partner).start()

    def pushed(j):
        for r in range(2):
            left_here(zsend.at[j, r], zx_s.at[j * 2 + r])

    parts = [project(0)]
    push(0)
    square = jnp.broadcast_to(jnp.sum(squares, axis=1, keepdims=True), (128, 128)).T
    ss_send[...] = square[0:8]
    remote(ss_send, ss_recv, zx_s.at[6], zx_r.at[6], partner).start()
    parts.append(project(1))
    pushed(0)
    push(1)
    parts.append(project(2))
    pushed(1)
    push(2)

    own_bit = (m // 2) % 2
    home = (m // 4) * 2 + m % 2

    @pl.when(own_bit == zh)
    def _():
        away = (1 - zh) * 8 + home
        remote(mid.at[away], resid, res_s.at[0], res_r.at[0], partner).start()
        resid[...] = mid[zh * 8 + home]

    spread_far(1)

    arrived(ss_recv, zx_r.at[6])
    square = ss_send[0:1] + ss_recv[0:1]
    norm = lax.rsqrt(square * (1.0 / 4096.0) + 1e-05)
    norm = jnp.broadcast_to(norm, (128, 128)).T
    norm = jnp.concatenate([norm, norm], axis=1)

    for d in (1, 3, 2):
        slot = ((y + d) % 4) * 4 + zh * 2 + c
        arrived(wso.at[slot], wso_r.at[slot])
    for d in range(4):
        slot = d * 4 + zh * 2 + c
        remote(wso.at[slot], wso.at[slot], wso_s.at[16 + d], wso_r.at[slot], sibling).start()

    def kv_block(j, slot, r):
        return kv.at[j, pl.ds(pl.multiple_of(slot * 128 + r * ROWS, ROWS), ROWS), :]

    def whole(j, r):
        arrived(zrecv.at[j, r], zx_r.at[j * 2 + r])
        rows = slice(r * ROWS, (r + 1) * ROWS)
        return ((parts[j][rows] + zrecv[j, r].astype(F32)) * norm[rows]).astype(BF16)

    for j in range(2):
        for r in range(2):
            block = kv_block(j, place, r)
            block[...] = whole(j, r)
            k = (j * 2 + r) * 8
            for d in (1, 3, 2):
                remote(block, block, kv_s.at[k + d], kv_r.at[k + place], y_peer(d)).start()
            remote(block, block, kv_s.at[k], kv_r.at[k + place], sibling).start()

    def pass_block(j, r):
        k = (j * 2 + r) * 8
        for d in (1, 3, 2):
            slot = ((y + d) % 4) * 2 + c
            block = kv_block(j, slot, r)
            arrived(block, kv_r.at[k + slot])
            remote(block, block, kv_s.at[k + 4 + d], kv_r.at[k + slot], sibling).start()

    def wait_block(j, r):
        for d in range(4):
            slot = d * 2 + 1 - c
            arrived(kv_block(j, slot, r), kv_r.at[(j * 2 + r) * 8 + slot])

    pass_block(0, 0)
    pass_block(0, 1)
    queries[0:ROWS] = whole(2, 0)
    queries[ROWS:] = whole(2, 1)

    for d in (1, 3, 2):
        slot = ((y + d) % 4) * 4 + (1 - zh) * 2 + c
        for k in range(2):
            arrived(half_slot(slot, k), wso_r.at[16 + slot * 2 + k])
    for d in range(4):
        slot = d * 4 + (1 - zh) * 2 + c
        remote(wso.at[slot], wso.at[slot], wso_s.at[20 + d], wso_r.at[slot], sibling).start()

    wait_block(0, 0)
    wait_block(0, 1)

    key_lane = lax.broadcasted_iota(jnp.int32, (128, 1024), 1)
    key_in = key_lane % 128
    key_place = (
        (key_lane // 256) * 256 + ((key_lane // 128) % 2) * 64 + (key_in // 64) * 128 + key_in % 64
    )
    query_row = lax.broadcasted_iota(jnp.int32, (128, 1024), 0)
    query_place = y * 256 + c * 64 + (query_row // 64) * 128 + query_row % 64
    allowed = key_place <= query_place
    spread, totals = [], []
    for hd in range(2):
        cols = slice(hd * HEAD_DIM, (hd + 1) * HEAD_DIM)
        scores = dot_nt(queries[:, cols], kv[0, :, cols]) * SCALE
        scores = jnp.where(allowed, scores, -1e30)
        top = jnp.max(scores, axis=1, keepdims=True)
        weights = jnp.where(allowed, jnp.exp(scores - top), 0.0)
        totals.append(jnp.sum(weights, axis=1, keepdims=True))
        spread.append(weights.astype(BF16))

    pass_block(1, 0)
    pass_block(1, 1)

    wait_block(1, 0)
    wait_block(1, 1)

    heads = []
    for hd in range(2):
        cols = slice(hd * HEAD_DIM, (hd + 1) * HEAD_DIM)
        heads.append(dot(spread[hd], kv[1, :, cols]) / totals[hd])
    ctx[...] = jnp.concatenate(heads, axis=1).astype(BF16)

    for d in range(4):
        for half in range(2):
            slot = d * 4 + half * 2 + 1 - c
            arrived(wso.at[slot], wso_r.at[slot])

    def self_part(t):
        rows = pl.ds(pl.multiple_of(half_of(t % 4) * ROWS, ROWS), ROWS)
        return dot(ctx[rows, :], wso[t]).astype(BF16)

    for other in z_order:
        for d in (2, 1, 3, 0):
            t = ((x + d) % 4) * 4 + other
            if d or other is not z_order[3]:
                send2[t] = self_part(t)
                remote(send2.at[t], recv2.at[m], rs2_s.at[t], rs2_r.at[m], peer(t)).start()
    recv2[m] = self_part(m)

    @pl.when(own_bit != zh)
    def _():
        arrived(resid, res_r.at[0])

    @pl.loop(1, 16)
    def _(i):
        s = (m + i) % 16
        arrived(recv2.at[s], rs2_r.at[s])

    sums = resid[...].astype(F32)
    for s in range(16):
        sums += recv2[s].astype(F32)
    out_ref[...] = sums.astype(BF16)

    @pl.loop(1, 16)
    def _(i):
        s = (m + i) % 16
        left_here(send1.at[s], rs1_s.at[s])
        left_here(send2.at[s], rs2_s.at[s])

    @pl.when(at_edge)
    def _():
        @pl.loop(0, 16)
        def _(i):
            left_here(ids.at[h], ids_s.at[8 + i])

        for i in range(2):
            left_here(offs.at[0], offs_s.at[i])

    @pl.loop(1, 8)
    def _(i):
        left_here(ids.at[h], ids_s.at[i])

    @pl.loop(0, 8)
    def _(i):
        @pl.when(i != 4)
        def _():
            left_here(wself.at[0], wself_s.at[i])
            for k in range(4):
                left_here(kv_block(0, 0, 0), kv_s.at[k * 8 + i])

    for i in (0, 1, 7, 8, 9, 11, 12, 13):
        left_here(half_slot(0, 0), wso_s.at[i])
    for i in (3, 4, 5, 16, 17, 18, 19, 20, 21, 22, 23):
        left_here(wso.at[0], wso_s.at[i])

    for i in (1, 2, 3, 5, 6, 7, 9, 10, 11, 13, 14, 15, 17, 18, 19):
        left_here(mid.at[0], ag_s.at[i])
    pushed(2)
    left_here(ss_send, zx_s.at[6])

    @pl.when(own_bit == zh)
    def _():
        left_here(resid, res_s.at[0])


def per_device(
    history_ids, latent_offsets, byte_table, w_query, w_key, w_value, w_out, norm_gain,
    w_self_query, w_self_key, w_self_value, w_self_out,
):
    vmem = pl.BlockSpec(memory_space=pltpu.VMEM)
    hbm = pl.BlockSpec(memory_space=pl.ANY)
    dma = pltpu.SemaphoreType.DMA
    scratch = [
        pltpu.VMEM((16, 4, 128), jnp.int32),
        pltpu.VMEM((2, 1, 64), jnp.int32),
        pltpu.VMEM((32, 128), BF16),
        pltpu.VMEM((32, 128), F32),
        pltpu.VMEM((256, 4096), BF16),
        pltpu.VMEM((4096, 256), BF16),
        pltpu.VMEM((4096, 256), BF16),
        pltpu.VMEM((4096, 256), BF16),
        pltpu.VMEM((8, 256, 256), BF16),
        pltpu.VMEM((8, 3, 256, 256), BF16),
        pltpu.VMEM((16, 256, 256), BF16),
        pltpu.VMEM((256, 256), BF16),
        pltpu.VMEM((256, 256), BF16),
        pltpu.VMEM((256, 256), BF16),
        pltpu.VMEM((128, 256), BF16),
        pltpu.VMEM((16, ROWS, WIDE), BF16),
        pltpu.VMEM((16, ROWS, WIDE), BF16),
        pltpu.VMEM((16, ROWS, WIDE), BF16),
        pltpu.VMEM((8, 128, WIDE), BF16),
        pltpu.VMEM((3, 2, ROWS, WIDE), BF16),
        pltpu.VMEM((3, 2, ROWS, WIDE), BF16),
        pltpu.VMEM((8, 128), F32),
        pltpu.VMEM((8, 128), F32),
        pltpu.VMEM((2, 1024, WIDE), BF16),
        pltpu.VMEM((128, WIDE), BF16),
        pltpu.VMEM((128, WIDE), BF16),
        pltpu.VMEM((16, ROWS, WIDE), BF16),
        pltpu.VMEM((16, ROWS, WIDE), BF16),
        pltpu.VMEM((ROWS, WIDE), BF16),
    ] + [dma((n,)) for n in (
        19, 24, 16, 8, 8, 24, 48, 16, 16, 20, 16, 7, 7, 32, 32, 16, 16, 1, 1, 2, 1
    )]
    return pl.pallas_call(
        kernel,
        out_shape=jax.ShapeDtypeStruct((ROWS, WIDE), BF16),
        in_specs=[hbm] * 12,
        out_specs=vmem,
        scratch_shapes=scratch,
        compiler_params=pltpu.CompilerParams(
            collective_id=0, has_side_effects=True, vmem_limit_bytes=56 * 1024 * 1024
        ),
        cost_estimate=pl.CostEstimate(
            flops=5_000_000_000, bytes_accessed=12_000_000, transcendentals=400_000
        ),
    )(
        history_ids.reshape(4, 128), latent_offsets.reshape(1, 64), norm_gain.reshape(32, 128),
        byte_table, w_query, w_key, w_value, w_out,
        w_self_query, w_self_key, w_self_value, w_self_out,
    )


def solution(mesh):
    return jax.shard_map(
        per_device,
        mesh=mesh,
        in_specs=(
            P("hist"),
            P("hist"),
            P(),
            P(None, "mp"),
            P(None, "mp"),
            P(None, "mp"),
            P("mp", None),
            P(),
            P("hist", "mp"),
            P("hist", "mp"),
            P("hist", "mp"),
            P("mp", "hist"),
        ),
        out_specs=P("hist", "mp"),
        check_vma=False,
    )
```

time: 77 us -> 69.7 us (0.905)
  Pallas kernels: 72.6 us -> 68.2 us
  local copies, waits for them, and re-layouts: 2.75 us -> 1.38 us
  other arithmetic: 1.34 us -> 0 us
    pallas_call x1, Pallas kernels: 72.6 us -> 68.2 us  [per_device(): pl.pallas_call(kernel, out_shape=jax.ShapeDtypeStruct((ROWS, WIDE), BF16)...]
    concatenate x1 -> x0, local copies, waits for them, and re-layouts: 1.37 us -> none  [per_device(): jnp.concatenate([history_ids.astype(F32), offsets, jnp.zeros((128,), F32)...]
    convert_element_type x2 -> x0, other arithmetic: 1.34 us -> none  [the longest x1 0.68 us: per_device(): history_ids.astype(F32)]
where the time goes in v3:
time: 69.7 us; the launch traced here: 69.6 us
  Pallas kernels  68.2 us (98%)
  local copies, waits for them, and re-layouts  1.38 us (2%)
    pallas_call x1, Pallas kernels, per_device(): pl.pallas_call(kernel, out_shape=jax.ShapeDtypeStruct((ROWS, WIDE), BF16)...  68.2 us

profile of v3, /device:TPU:1, one launch (start us, length us, event | category | flops | bytes accessed | tf_op | source)
XLA Modules:
  0.0 69.6 jit_solution(9214949801035206185)
XLA Ops:
  0.0 68.2 %shard_map.118 = bf16[64,256]{1,0:T(8,128)(2,1)} custom-call(s32[4,128]{1,0:T(4,128)} %bitcast.4, s32[1,64]{1,0:T(1,128)} %bitcast.5, bf16[32,128]{1,0:T(8,128)(2,1)} %bitcast.3, bf16[256,4096]{1,0:T(8,128)(2,1)} %tab_hbm.1, bf16[4096,256]{1,0:T(8,128)(2,1)} %wq_hbm.1, bf16[4096,256]{1,0:T(8,128)(2,1)} %wk_hbm.1, bf16[4096,256]{1,0:T(8,128)(2,1)} %wv_hbm.1, ...), custom_call_target="tpu_custom_call" | custom-call | flops 5000000000 | bytes 12000000 | tf_op jit(solution)/shard_map/pallas_call | solution.py:583
  68.2 1.4 %copy.14 = bf16[64,256]{1,0:T(8,128)(2,1)} copy(bf16[64,256]{1,0:T(8,128)(2,1)} %shard_map.118) | data formatting | bytes 65536

commit v4 on v3

--- a/solution.py
+++ b/solution.py
@@ -321,30 +321,39 @@
     local[10].wait()
     gain_rows[...] = gains[...].astype(F32)
 
-    @pl.loop(4, 16)
-    def _(i):
-        t = (m - m % 4 + i) % 16
-        arrived(mid.at[t], ag_r.at[t])
-
-    squares = jnp.zeros((128, 128), F32)
-    for b in range(8):
-        rows = jnp.concatenate([mid[b], mid[8 + b]], axis=0).astype(F32)
-        squares += rows[:, :128] * rows[:, :128] + rows[:, 128:] * rows[:, 128:]
-        first = ((b // 2) * 4 + zh * 2 + b % 2) * 2
-        gain = [gain_rows[pl.ds(first + i, 1), :] for i in range(2)]
-        left[b] = (rows * jnp.concatenate(gain, axis=1)).astype(BF16)
-
     for d in range(4):
         slot = d * 2 + 1 - c
         arrived(wself.at[slot], wself_r.at[slot])
+
+    squares = jnp.zeros((128, 128), F32)
+    key_part = jnp.zeros((128, WIDE), F32)
+    for other in (zl, *order):
+        for e in range(2):
+            b = e * 4 + other
+            for r in range(2):
+
+                @pl.when(x != e + 2 * r)
+                def _(t=r * 8 + b):
+                    arrived(mid.at[t], ag_r.at[t])
+
+            rows = jnp.concatenate([mid[b], mid[8 + b]], axis=0).astype(F32)
+            squares += rows[:, :128] * rows[:, :128] + rows[:, 128:] * rows[:, 128:]
+            first = ((b // 2) * 4 + zh * 2 + b % 2) * 2
+            gain = [gain_rows[pl.ds(first + i, 1), :] for i in range(2)]
+            scaled = (rows * jnp.concatenate(gain, axis=1)).astype(BF16)
+            left[b] = scaled
+            key_part += dot(scaled, wself[b, 0])
+
+    def keep(j, part):
+        zsend[j, 0] = part[:ROWS].astype(BF16)
+        zsend[j, 1] = part[ROWS:].astype(BF16)
+        return part
 
     def project(j):
         part = dot(left[0], wself[0, j])
         for b in range(1, 8):
             part += dot(left[b], wself[b, j])
-        zsend[j, 0] = part[:ROWS].astype(BF16)
-        zsend[j, 1] = part[ROWS:].astype(BF16)
-        return part
+        return keep(j, part)
 
     def push(j):
         for r in range(2):
@@ -355,17 +364,14 @@
         for r in range(2):
             left_here(zsend.at[j, r], zx_s.at[j * 2 + r])
 
-    parts = [project(0)]
+    parts = [keep(0, key_part)]
     push(0)
     square = jnp.broadcast_to(jnp.sum(squares, axis=1, keepdims=True), (128, 128)).T
     ss_send[...] = square[0:8]
     remote(ss_send, ss_recv, zx_s.at[6], zx_r.at[6], partner).start()
     parts.append(project(1))
-    pushed(0)
     push(1)
     parts.append(project(2))
-    pushed(1)
-    push(2)
 
     own_bit = (m // 2) % 2
     home = (m // 4) * 2 + m % 2
@@ -407,6 +413,8 @@
             for d in (1, 3, 2):
                 remote(block, block, kv_s.at[k + d], kv_r.at[k + place], y_peer(d)).start()
             remote(block, block, kv_s.at[k], kv_r.at[k + place], sibling).start()
+        if j == 0:
+            push(2)
 
     def pass_block(j, r):
         k = (j * 2 + r) * 8
@@ -532,6 +540,8 @@
 
     for i in (1, 2, 3, 5, 6, 7, 9, 10, 11, 13, 14, 15, 17, 18, 19):
         left_here(mid.at[0], ag_s.at[i])
+    pushed(0)
+    pushed(1)
     pushed(2)
     left_here(ss_send, zx_s.at[6])
 

time: 69.7 us -> 67.6 us (0.970)
  Pallas kernels: 68.2 us -> 66.1 us
    pallas_call x1, Pallas kernels: 68.2 us -> 66.1 us  [per_device(): pl.pallas_call(kernel, out_shape=jax.ShapeDtypeStruct((ROWS, WIDE), BF16)...]
where the time goes in v4:
time: 67.6 us; the launch traced here: 67.5 us
  Pallas kernels  66.1 us (98%)
  local copies, waits for them, and re-layouts  1.38 us (2%)
    pallas_call x1, Pallas kernels, per_device(): pl.pallas_call(kernel, out_shape=jax.ShapeDtypeStruct((ROWS, WIDE), BF16)...  66.1 us
    unnamed x1, local copies, waits for them, and re-layouts  1.38 us

profile of v4, /device:TPU:1, one launch (start us, length us, event | category | flops | bytes accessed | tf_op | source)
XLA Modules:
  0.0 67.5 jit_solution(17620496949317795872)
XLA Ops:
  0.0 66.1 %shard_map.118 = bf16[64,256]{1,0:T(8,128)(2,1)} custom-call(s32[4,128]{1,0:T(4,128)} %bitcast.4, s32[1,64]{1,0:T(1,128)} %bitcast.5, bf16[32,128]{1,0:T(8,128)(2,1)} %bitcast.3, bf16[256,4096]{1,0:T(8,128)(2,1)} %tab_hbm.1, bf16[4096,256]{1,0:T(8,128)(2,1)} %wq_hbm.1, bf16[4096,256]{1,0:T(8,128)(2,1)} %wk_hbm.1, bf16[4096,256]{1,0:T(8,128)(2,1)} %wv_hbm.1, ...), custom_call_target="tpu_custom_call" | custom-call | flops 5000000000 | bytes 12000000 | tf_op jit(solution)/shard_map/pallas_call | solution.py:593
  66.1 1.4 %copy.14 = bf16[64,256]{1,0:T(8,128)(2,1)} copy(bf16[64,256]{1,0:T(8,128)(2,1)} %shard_map.118) | data formatting | bytes 65536

commit v5 on v4

--- a/solution.py
+++ b/solution.py
@@ -257,7 +257,7 @@
     turn = 3 - 2 * (zl % 2)
     z_order = [(zl + e) % 4 for e in (2, turn, 4 - turn, 0)]
     for other in z_order:
-        for e in range(2):
+        for e in (1, 0):
             b = ((x + e) % 2) * 4 + other
             part = dot(ctx[...], wo[b]).astype(BF16)
             send1[b] = part[:ROWS]
@@ -289,14 +289,15 @@
     mid[m] = (total + sums).astype(BF16)
 
     order = (zl + 1 - 2 * (zl % 2), jnp.where(zl < 2, 2, 1), jnp.where(zl < 2, 3, 0))
+    for d in (1, 3, 2):
+        remote(
+            mid.at[m], mid.at[m], ag_s.at[4 + d], ag_r.at[m], (h, ((x + d) % 4) * 4 + zl)
+        ).start()
     for e, other in enumerate(order):
         remote(
             mid.at[m], mid.at[m], ag_s.at[1 + e], ag_r.at[m], (h, x * 4 + other)
         ).start()
-    for d in (1, 3, 2):
-        remote(
-            mid.at[m], mid.at[m], ag_s.at[4 + d], ag_r.at[m], (h, ((x + d) % 4) * 4 + zl)
-        ).start()
+
     for d in (1, 3, 2):
         remote(wso.at[h], wso.at[h], wso_s.at[2 + d], wso_r.at[h], y_peer(d)).start()
     spread_far(0)

time: 67.6 us -> 67.3 us (level)
  no operation moved by 1% of the time
where the time goes in v5:
time: 67.3 us; the launch traced here: 67.2 us
  Pallas kernels  65.8 us (98%)
  local copies, waits for them, and re-layouts  1.38 us (2%)
    pallas_call x1, Pallas kernels, per_device(): pl.pallas_call(kernel, out_shape=jax.ShapeDtypeStruct((ROWS, WIDE), BF16)...  65.8 us
    unnamed x1, local copies, waits for them, and re-layouts  1.38 us

profile of v5, /device:TPU:1, one launch (start us, length us, event | category | flops | bytes accessed | tf_op | source)
XLA Modules:
  0.0 67.2 jit_solution(17728144526715338995)
XLA Ops:
  0.0 65.8 %shard_map.118 = bf16[64,256]{1,0:T(8,128)(2,1)} custom-call(s32[4,128]{1,0:T(4,128)} %bitcast.4, s32[1,64]{1,0:T(1,128)} %bitcast.5, bf16[32,128]{1,0:T(8,128)(2,1)} %bitcast.3, bf16[256,4096]{1,0:T(8,128)(2,1)} %tab_hbm.1, bf16[4096,256]{1,0:T(8,128)(2,1)} %wq_hbm.1, bf16[4096,256]{1,0:T(8,128)(2,1)} %wk_hbm.1, bf16[4096,256]{1,0:T(8,128)(2,1)} %wv_hbm.1, ...), custom_call_target="tpu_custom_call" | custom-call | flops 5000000000 | bytes 12000000 | tf_op jit(solution)/shard_map/pallas_call | solution.py:594
  65.8 1.4 %copy.14 = bf16[64,256]{1,0:T(8,128)(2,1)} copy(bf16[64,256]{1,0:T(8,128)(2,1)} %shard_map.118) | data formatting | bytes 65536

commit v6 on v5

--- a/solution.py
+++ b/solution.py
@@ -278,25 +278,23 @@
         tab[:, pl.ds(pl.multiple_of(own_block * WIDE, WIDE), WIDE)],
     )
 
-    @pl.loop(1, 16)
-    def _(i):
-        s = (m + i) % 16
-        arrived(recv1.at[s], rs1_r.at[s])
-
-    sums = recv1[0].astype(F32)
-    for s in range(1, 16):
-        sums += recv1[s].astype(F32)
+    sums = jnp.zeros((ROWS, WIDE), F32)
+    for other in reversed(z_order):
+        for d in (0, 1, 3, 2):
+            s = ((x + d) % 4) * 4 + other
+            if d or other is not z_order[3]:
+                arrived(recv1.at[s], rs1_r.at[s])
+            sums += recv1[s].astype(F32)
     mid[m] = (total + sums).astype(BF16)
 
     order = (zl + 1 - 2 * (zl % 2), jnp.where(zl < 2, 2, 1), jnp.where(zl < 2, 3, 0))
+    remote(mid.at[m], mid.at[m], ag_s.at[1], ag_r.at[m], (h, x * 4 + order[0])).start()
     for d in (1, 3, 2):
         remote(
             mid.at[m], mid.at[m], ag_s.at[4 + d], ag_r.at[m], (h, ((x + d) % 4) * 4 + zl)
         ).start()
-    for e, other in enumerate(order):
-        remote(
-            mid.at[m], mid.at[m], ag_s.at[1 + e], ag_r.at[m], (h, x * 4 + other)
-        ).start()
+    for e in (1, 2):
+        remote(mid.at[m], mid.at[m], ag_s.at[1 + e], ag_r.at[m], (h, x * 4 + order[e])).start()
 
     for d in (1, 3, 2):
         remote(wso.at[h], wso.at[h], wso_s.at[2 + d], wso_r.at[h], y_peer(d)).start()
@@ -497,14 +495,13 @@
     def _():
         arrived(resid, res_r.at[0])
 
-    @pl.loop(1, 16)
-    def _(i):
-        s = (m + i) % 16
-        arrived(recv2.at[s], rs2_r.at[s])
-
     sums = resid[...].astype(F32)
-    for s in range(16):
-        sums += recv2[s].astype(F32)
+    for other in reversed(z_order):
+        for d in (0, 1, 3, 2):
+            s = ((x + d) % 4) * 4 + other
+            if d or other is not z_order[3]:
+                arrived(recv2.at[s], rs2_r.at[s])
+            sums += recv2[s].astype(F32)
     out_ref[...] = sums.astype(BF16)
 
     @pl.loop(1, 16)

time: 67.3 us -> 67.3 us (level)
  no operation moved by 1% of the time
where the time goes in v6:
time: 67.3 us; the launch traced here: 67.2 us
  Pallas kernels  65.8 us (98%)
  local copies, waits for them, and re-layouts  1.38 us (2%)
    pallas_call x1, Pallas kernels, per_device(): pl.pallas_call(kernel, out_shape=jax.ShapeDtypeStruct((ROWS, WIDE), BF16)...  65.8 us
    unnamed x1, local copies, waits for them, and re-layouts  1.38 us

profile of v6, /device:TPU:1, one launch (start us, length us, event | category | flops | bytes accessed | tf_op | source)
XLA Modules:
  0.0 67.2 jit_solution(14637591754701970281)
XLA Ops:
  0.0 65.8 %shard_map.118 = bf16[64,256]{1,0:T(8,128)(2,1)} custom-call(s32[4,128]{1,0:T(4,128)} %bitcast.4, s32[1,64]{1,0:T(1,128)} %bitcast.5, bf16[32,128]{1,0:T(8,128)(2,1)} %bitcast.3, bf16[256,4096]{1,0:T(8,128)(2,1)} %tab_hbm.1, bf16[4096,256]{1,0:T(8,128)(2,1)} %wq_hbm.1, bf16[4096,256]{1,0:T(8,128)(2,1)} %wk_hbm.1, bf16[4096,256]{1,0:T(8,128)(2,1)} %wv_hbm.1, ...), custom_call_target="tpu_custom_call" | custom-call | flops 5000000000 | bytes 12000000 | tf_op jit(solution)/shard_map/pallas_call | solution.py:591
  65.8 1.4 %copy.14 = bf16[64,256]{1,0:T(8,128)(2,1)} copy(bf16[64,256]{1,0:T(8,128)(2,1)} %shard_map.118) | data formatting | bytes 65536
